TPU v7x, 256 devices: a whole 4x4x8 slice. The times are simulated.
256 devices in a mesh: prow: 8 (over y_hi, x), pcol: 32 (over z, y_lo, core).
Axes of the slice: x: 4, y: 4 (y_hi: 2, y_lo: 2; y = y_hi * 2 + y_lo), z: 8, core: 2. Of those that a mesh axis runs over, the one named last changes fastest.
Arguments:
- factor_panels: float32 [8, 4096, 512], P('prow', 'pcol'), may hold values from -0.046875 to 0.046875
- diag_inverse: float32 [8, 512, 512], P('prow'), as said below
- block_lists: int32 [8, 7], replicated, may hold values from 1 to 8, as said below
- parent: int32 [8], replicated, may hold values from 1 to 8, as said below
Outputs:
- inverse_blocks: float32 [8, 4096, 512], P('prow', 'pcol')
Inputs may be any that keep to these rules, and one draw needn't show every extreme that they name: `block_lists`: row K lists in rising order the supernodes whose block rows are nonzero in factor column K, padded at the end with 8; every listed supernode is an ancestor of K, parent[K] is listed, and every other listed supernode is also listed for parent[K]; the last row is all padding. parent[K] > K; the last supernode is the root and has the value 8. `diag_inverse`: each block is symmetric.
All inputs are finite; a program needn't handle non-finite values.
Results may differ from a plain program's by a relative error of at most 0.0001.
Values sent between devices are 32-bit elements; how exact they have to be, the bound alone decides.
A program may use at most 64 MiB of HBM per device.

v0:
```python
import jax
import jax.numpy as jnp
from jax import lax
from jax.sharding import PartitionSpec as P


def pattern_of(block_lists, parent, target, node_ids):
    listed = jnp.any(block_lists[target][:, None] == node_ids[None, :], axis=0)
    return jnp.logical_or(listed, parent[target] == node_ids).astype(jnp.float32)


def shards(factor_panels, diag_inverse, block_lists, parent):
    grid_row = lax.axis_index("prow")
    grid_col = lax.axis_index("pcol")
    share_rows = factor_panels.shape[1]
    block_width = factor_panels.shape[2]
    node_count = block_lists.shape[0]
    shares = block_width // share_rows
    my_block = grid_col // shares
    my_share = grid_col % shares
    node_ids = jnp.arange(node_count, dtype=jnp.int32)
    local_factor = factor_panels[0]
    whole_row = lax.all_gather(local_factor, "pcol", axis=0, tiled=True)
    diag_local = lax.dynamic_slice_in_dim(diag_inverse[0], my_share * share_rows, share_rows, 0)
    inverse = jnp.zeros((share_rows, block_width), jnp.float32)
    for target in range(node_count - 1, -1, -1):
        pattern_mask = pattern_of(block_lists, parent, target, node_ids)
        own_weight = jnp.sum(jnp.where(node_ids == grid_row, pattern_mask, 0.0))
        block_weight = jnp.sum(jnp.where(node_ids == my_block, pattern_mask, 0.0))
        factor_block = whole_row[target * block_width : (target + 1) * block_width]
        panel = factor_block * own_weight
        product = jnp.dot(inverse, panel, precision=lax.Precision.HIGHEST)
        summed = lax.psum(product, "prow")
        column_rows = -summed * block_weight
        split_cols = jnp.transpose(column_rows.reshape(share_rows, shares, share_rows), (1, 0, 2))
        outgoing = jnp.broadcast_to(split_cols[None], (node_count, shares, share_rows, share_rows))
        outgoing = outgoing.reshape(node_count * shares * share_rows, share_rows)
        incoming = lax.all_to_all(outgoing, "pcol", split_axis=0, concat_axis=0, tiled=True)
        mirror_block = lax.dynamic_slice_in_dim(
            incoming, grid_row * shares * share_rows, shares * share_rows, 0
        )
        mirror_rows = mirror_block.T
        local_term = jnp.dot(mirror_rows, panel, precision=lax.Precision.HIGHEST)
        diagonal = lax.psum(local_term, "prow")
        is_row = grid_row == target
        in_column = my_block == target
        updated = jnp.where(is_row, column_rows, inverse)
        updated = jnp.where(in_column, mirror_rows, updated)
        updated = jnp.where(jnp.logical_and(is_row, in_column), diag_local - diagonal, updated)
        inverse = updated
    return inverse[None]


def solution(mesh):
    placed = (P("prow", "pcol", None), P("prow", None, None), P(), P())
    return jax.shard_map(
        shards, mesh=mesh, in_specs=placed, out_specs=P("prow", "pcol", None), check_vma=False
    )
```

profile of v0, /device:TPU:41, one launch (start us, length us, event | category | flops | bytes accessed | tf_op | source)
XLA Modules:
  0.0 2020.8 jit_solution(9255409412016598542)
XLA Ops:
  7.3 1.6 fusion.91
  11.3 72.1 %all-gather.3.cloned.1.call-done = f32[1,4096,512]{2,1,0:T(8,128)} async-done(((f32[1,128,512]{2,1,0:T(8,128)}), f32[1,4096,512]{2,1,0:T(8,128)}) %all-gather.3.cloned.1.call-update) | async-done | bytes 8388624 | tf_op jit(solution)/shard_map/all_gather | solution.py:23
  83.4 3.3 fusion.10
  86.7 83.9 %all-reduce.17.cloned.1.call-done = f32[128,512]{1,0:T(8,128)} async-done(((f32[128,512]{1,0:T(8,128)}), f32[128,512]{1,0:T(8,128)}) %all-reduce.17.cloned.1.call-update) | async-done | bytes 262160 | tf_op jit(solution)/shard_map/psum | solution.py:33
  170.6 1.6 negate_multiply_fusion.7
  172.4 1.6 broadcast_in_dim.41
  174.1 14.3 all-to-all-start
  188.5 50.3 %all-to-all-done = f32[32,128,128]{1,2,0:T(8,128)S(1)} async-done(((f32[32,128,128]{1,2,0:T(8,128)}), f32[32,128,128]{1,2,0:T(8,128)S(1)}, u32[]{:S(2)}, u32[]{:S(2)}) %all-to-all-start) | async-done | bytes 2097184 | tf_op jit(solution)/shard_map/all_to_all | solution.py:38
  239.0 1.4 copy-done.1
  240.4 3.3 fusion.8
  245.0 76.7 %all-reduce.19.cloned.1.call-done = f32[128,512]{1,0:T(8,128)} async-done(((f32[128,512]{1,0:T(8,128)}), f32[128,512]{1,0:T(8,128)}) %all-reduce.19.cloned.1.call-update) | async-done | bytes 262160 | tf_op jit(solution)/shard_map/psum | solution.py:44
  321.7 1.7 fusion.64
  323.5 3.4 fusion.14
  326.9 87.7 %all-reduce.21.cloned.1.call-done = f32[128,512]{1,0:T(8,128)} async-done(((f32[128,512]{1,0:T(8,128)}), f32[128,512]{1,0:T(8,128)}) %all-reduce.21.cloned.1.call-update) | async-done | bytes 262160 | tf_op jit(solution)/shard_map/psum | solution.py:33
  414.6 1.6 negate_multiply_fusion.6
  416.7 64.5 %all_to_all.96 = f32[32,128,128]{1,2,0:T(8,128)S(1)} all-to-all(f32[32,128,128]{1,2,0:T(8,128)S(1)} %bitcast.181), channel_id=1, replica_groups=mesh['prow'=8,'pcol'=32] {'pcol'}, dimensions={0} | all-to-all | bytes 4194304 | tf_op jit(solution)/shard_map/all_to_all | solution.py:38
  481.4 3.4 fusion.12
  486.2 76.7 %all-reduce.23.cloned.1.call-done = f32[128,512]{1,0:T(8,128)} async-done(((f32[128,512]{1,0:T(8,128)}), f32[128,512]{1,0:T(8,128)}) %all-reduce.23.cloned.1.call-update) | async-done | bytes 262160 | tf_op jit(solution)/shard_map/psum | solution.py:44
  562.8 1.8 fusion.63
  565.3 3.2 fusion.18
  568.6 87.7 %all-reduce.25.cloned.1.call-done = f32[128,512]{1,0:T(8,128)} async-done(((f32[128,512]{1,0:T(8,128)}), f32[128,512]{1,0:T(8,128)}) %all-reduce.25.cloned.1.call-update) | async-done | bytes 262160 | tf_op jit(solution)/shard_map/psum | solution.py:33
  656.4 1.5 negate_multiply_fusion.5
  658.4 64.5 %all_to_all.97 = f32[32,128,128]{1,2,0:T(8,128)S(1)} all-to-all(f32[32,128,128]{1,2,0:T(8,128)S(1)} %bitcast.182), channel_id=1, replica_groups=mesh['prow'=8,'pcol'=32] {'pcol'}, dimensions={0} | all-to-all | bytes 4194304 | tf_op jit(solution)/shard_map/all_to_all | solution.py:38
  723.1 3.2 fusion.16
  726.4 1.3 select_reduce_fusion.8
  727.7 76.7 %all-reduce.27.cloned.1.call-done = f32[128,512]{1,0:T(8,128)} async-done(((f32[128,512]{1,0:T(8,128)}), f32[128,512]{1,0:T(8,128)}) %all-reduce.27.cloned.1.call-update) | async-done | bytes 262160 | tf_op jit(solution)/shard_map/psum | solution.py:44
  804.4 1.8 fusion.62
  806.2 3.4 fusion.22
  809.6 87.6 %all-reduce.29.cloned.1.call-done = f32[128,512]{1,0:T(8,128)} async-done(((f32[128,512]{1,0:T(8,128)}), f32[128,512]{1,0:T(8,128)}) %all-reduce.29.cloned.1.call-update) | async-done | bytes 262160 | tf_op jit(solution)/shard_map/psum | solution.py:33
  897.2 1.6 negate_multiply_fusion.4
  899.3 64.5 %all_to_all.98 = f32[32,128,128]{1,2,0:T(8,128)S(1)} all-to-all(f32[32,128,128]{1,2,0:T(8,128)S(1)} %bitcast.183), channel_id=1, replica_groups=mesh['prow'=8,'pcol'=32] {'pcol'}, dimensions={0} | all-to-all | bytes 4194304 | tf_op jit(solution)/shard_map/all_to_all | solution.py:38
  964.0 3.4 fusion.20
  968.9 76.5 %all-reduce.31.cloned.1.call-done = f32[128,512]{1,0:T(8,128)} async-done(((f32[128,512]{1,0:T(8,128)}), f32[128,512]{1,0:T(8,128)}) %all-reduce.31.cloned.1.call-update) | async-done | bytes 262160 | tf_op jit(solution)/shard_map/psum | solution.py:44
  1045.4 1.8 fusion.61
  1047.9 3.3 fusion.26
  1051.3 87.7 %all-reduce.33.cloned.1.call-done = f32[128,512]{1,0:T(8,128)} async-done(((f32[128,512]{1,0:T(8,128)}), f32[128,512]{1,0:T(8,128)}) %all-reduce.33.cloned.1.call-update) | async-done | bytes 262160 | tf_op jit(solution)/shard_map/psum | solution.py:33
  1139.0 1.5 negate_multiply_fusion.3
  1141.0 64.5 %all_to_all.99 = f32[32,128,128]{1,2,0:T(8,128)S(1)} all-to-all(f32[32,128,128]{1,2,0:T(8,128)S(1)} %bitcast.184), channel_id=1, replica_groups=mesh['prow'=8,'pcol'=32] {'pcol'}, dimensions={0} | all-to-all | bytes 4194304 | tf_op jit(solution)/shard_map/all_to_all | solution.py:38
  1205.7 3.3 fusion.24
  1209.1 1.4 select_reduce_fusion.4
  1210.5 76.6 %all-reduce.35.cloned.1.call-done = f32[128,512]{1,0:T(8,128)} async-done(((f32[128,512]{1,0:T(8,128)}), f32[128,512]{1,0:T(8,128)}) %all-reduce.35.cloned.1.call-update) | async-done | bytes 262160 | tf_op jit(solution)/shard_map/psum | solution.py:44
  1287.1 1.8 fusion.60
  1288.9 3.4 fusion.30
  1292.4 87.7 %all-reduce.37.cloned.1.call-done = f32[128,512]{1,0:T(8,128)} async-done(((f32[128,512]{1,0:T(8,128)}), f32[128,512]{1,0:T(8,128)}) %all-reduce.37.cloned.1.call-update) | async-done | bytes 262160 | tf_op jit(solution)/shard_map/psum | solution.py:33
  1380.1 1.6 negate_multiply_fusion.2
  1382.2 64.5 %all_to_all.100 = f32[32,128,128]{1,2,0:T(8,128)S(1)} all-to-all(f32[32,128,128]{1,2,0:T(8,128)S(1)} %bitcast.185), channel_id=1, replica_groups=mesh['prow'=8,'pcol'=32] {'pcol'}, dimensions={0} | all-to-all | bytes 4194304 | tf_op jit(solution)/shard_map/all_to_all | solution.py:38
  1446.8 3.4 fusion.28
  1450.4 1.3 select_reduce_fusion.2
  1451.7 76.5 %all-reduce.39.cloned.1.call-done = f32[128,512]{1,0:T(8,128)} async-done(((f32[128,512]{1,0:T(8,128)}), f32[128,512]{1,0:T(8,128)}) %all-reduce.39.cloned.1.call-update) | async-done | bytes 262160 | tf_op jit(solution)/shard_map/psum | solution.py:44
  1528.2 1.8 fusion.59
  1530.7 3.4 fusion.34
  1534.2 87.7 %all-reduce.41.cloned.1.call-done = f32[128,512]{1,0:T(8,128)} async-done(((f32[128,512]{1,0:T(8,128)}), f32[128,512]{1,0:T(8,128)}) %all-reduce.41.cloned.1.call-update) | async-done | bytes 262160 | tf_op jit(solution)/shard_map/psum | solution.py:33
  1621.9 1.5 negate_multiply_fusion.1
  1623.9 64.5 %all_to_all.101 = f32[32,128,128]{1,2,0:T(8,128)S(1)} all-to-all(f32[32,128,128]{1,2,0:T(8,128)S(1)} %bitcast.186), channel_id=1, replica_groups=mesh['prow'=8,'pcol'=32] {'pcol'}, dimensions={0} | all-to-all | bytes 4194304 | tf_op jit(solution)/shard_map/all_to_all | solution.py:38
  1688.6 3.4 fusion.32
  1693.3 76.8 %all-reduce.43.cloned.1.call-done = f32[128,512]{1,0:T(8,128)} async-done(((f32[128,512]{1,0:T(8,128)}), f32[128,512]{1,0:T(8,128)}) %all-reduce.43.cloned.1.call-update) | async-done | bytes 262160 | tf_op jit(solution)/shard_map/psum | solution.py:44
  1770.0 1.7 fusion.58
  1772.5 3.4 fusion.38
  1775.9 87.7 %all-reduce.45.cloned.1.call-done = f32[128,512]{1,0:T(8,128)} async-done(((f32[128,512]{1,0:T(8,128)}), f32[128,512]{1,0:T(8,128)}) %all-reduce.45.cloned.1.call-update) | async-done | bytes 262160 | tf_op jit(solution)/shard_map/psum | solution.py:33
  1863.6 1.6 negate_multiply_fusion
  1865.7 64.5 %all_to_all.102 = f32[32,128,128]{1,2,0:T(8,128)S(1)} all-to-all(f32[32,128,128]{1,2,0:T(8,128)S(1)} %bitcast.187), channel_id=1, replica_groups=mesh['prow'=8,'pcol'=32] {'pcol'}, dimensions={0} | all-to-all | bytes 4194304 | tf_op jit(solution)/shard_map/all_to_all | solution.py:38
  1930.4 3.4 fusion.36
  1933.8 78.0 %all-reduce.47.cloned.1.call-done = f32[128,512]{1,0:T(8,128)} async-done(((f32[128,512]{1,0:T(8,128)}), f32[128,512]{1,0:T(8,128)}) %all-reduce.47.cloned.1.call-update) | async-done | bytes 262160 | tf_op jit(solution)/shard_map/psum | solution.py:44
  2011.8 2.5 fusion.57
  (92 shorter events, 17.2 us)
Async XLA Ops:
  6.5 76.8 %all-gather.3.cloned.1.call-start = ((), (), s32[]{:S(2)}) async-start(), calls=%async_computation.24 | async-start | bytes 8650752 | tf_op jit(solution)/shard_map/all_gather | solution.py:23
  7.3 163.4 %all-reduce.17.cloned.1.call-start = ((), (), s32[]{:S(2)}) async-start(), calls=%async_computation.8 | async-start | bytes 524288 | tf_op jit(solution)/shard_map/psum | solution.py:33
  174.1 64.7 %all-to-all-start = ((f32[32,128,128]{1,2,0:T(8,128)}), f32[32,128,128]{1,2,0:T(8,128)S(1)}, u32[]{:S(2)}, u32[]{:S(2)}) async-start(f32[32,128,128]{1,2,0:T(8,128)} %bitcast.180), calls=%async_computation | async-start | bytes 4194304 | tf_op jit(solution)/shard_map/all_to_all | solution.py:38
  188.4 133.4 %all-reduce.19.cloned.1.call-start = ((), (), s32[]{:S(2)}) async-start(), calls=%async_computation.9 | async-start | bytes 524288 | tf_op jit(solution)/shard_map/psum | solution.py:44
  188.4 133.3 %copy-start = (f32[1,512,512]{2,1,0:T(8,128)S(1)}, f32[1,512,512]{2,1,0:T(8,128)}, u32[]{:S(2)}) copy-start(f32[1,512,512]{2,1,0:T(8,128)} %param.5) | copy-start | bytes 3145732
  188.4 133.3 %copy-start.8 = (f32[128,512]{1,0:T(8,128)S(1)}, f32[128,512]{1,0:T(8,128)}, u32[]{:S(2)}) copy-start(f32[128,512]{1,0:T(8,128)} %all-reduce.17.cloned.1.call-done) | copy-start | bytes 786436
  239.0 1.4 copy-start.1
  243.7 170.9 %all-reduce.21.cloned.1.call-start = ((), (), s32[]{:S(2)}) async-start(), calls=%async_computation.10 | async-start | bytes 524288 | tf_op jit(solution)/shard_map/psum | solution.py:33
  326.9 236.0 %all-reduce.23.cloned.1.call-start = ((), (), s32[]{:S(2)}) async-start(), calls=%async_computation.11 | async-start | bytes 524288 | tf_op jit(solution)/shard_map/psum | solution.py:44
  484.8 171.6 %all-reduce.25.cloned.1.call-start = ((), (), s32[]{:S(2)}) async-start(), calls=%async_computation.12 | async-start | bytes 524288 | tf_op jit(solution)/shard_map/psum | solution.py:33
  564.6 0.7 copy-start.4
  568.6 235.8 %all-reduce.27.cloned.1.call-start = ((), (), s32[]{:S(2)}) async-start(), calls=%async_computation.13 | async-start | bytes 524288 | tf_op jit(solution)/shard_map/psum | solution.py:44
  726.3 170.9 %all-reduce.29.cloned.1.call-start = ((), (), s32[]{:S(2)}) async-start(), calls=%async_computation.14 | async-start | bytes 524288 | tf_op jit(solution)/shard_map/psum | solution.py:33
  809.6 235.9 %all-reduce.31.cloned.1.call-start = ((), (), s32[]{:S(2)}) async-start(), calls=%async_computation.15 | async-start | bytes 524288 | tf_op jit(solution)/shard_map/psum | solution.py:44
  967.4 171.6 %all-reduce.33.cloned.1.call-start = ((), (), s32[]{:S(2)}) async-start(), calls=%async_computation.16 | async-start | bytes 524288 | tf_op jit(solution)/shard_map/psum | solution.py:33
  1047.2 0.7 copy-start.5
  1051.3 235.9 %all-reduce.35.cloned.1.call-start = ((), (), s32[]{:S(2)}) async-start(), calls=%async_computation.17 | async-start | bytes 524288 | tf_op jit(solution)/shard_map/psum | solution.py:44
  1209.1 171.0 %all-reduce.37.cloned.1.call-start = ((), (), s32[]{:S(2)}) async-start(), calls=%async_computation.18 | async-start | bytes 524288 | tf_op jit(solution)/shard_map/psum | solution.py:33
  1292.3 235.9 %all-reduce.39.cloned.1.call-start = ((), (), s32[]{:S(2)}) async-start(), calls=%async_computation.19 | async-start | bytes 524288 | tf_op jit(solution)/shard_map/psum | solution.py:44
  1450.2 171.7 %all-reduce.41.cloned.1.call-start = ((), (), s32[]{:S(2)}) async-start(), calls=%async_computation.20 | async-start | bytes 524288 | tf_op jit(solution)/shard_map/psum | solution.py:33
  1530.0 0.7 copy-start.2
  1534.1 235.9 %all-reduce.43.cloned.1.call-start = ((), (), s32[]{:S(2)}) async-start(), calls=%async_computation.21 | async-start | bytes 524288 | tf_op jit(solution)/shard_map/psum | solution.py:44
  1688.4 81.7 %copy-start.3 = (f32[128,512]{1,0:T(8,128)S(1)}, f32[128,512]{1,0:T(8,128)}, u32[]{:S(2)}) copy-start(f32[128,512]{1,0:T(8,128)} %copy-done.2) | copy-start | bytes 786436
  1692.0 171.7 %all-reduce.45.cloned.1.call-start = ((), (), s32[]{:S(2)}) async-start(), calls=%async_computation.22 | async-start | bytes 524288 | tf_op jit(solution)/shard_map/psum | solution.py:33
  1771.8 0.7 copy-start.6
  1775.9 236.0 %all-reduce.47.cloned.1.call-start = ((), (), s32[]{:S(2)}) async-start(), calls=%async_computation.23 | async-start | bytes 524288 | tf_op jit(solution)/shard_map/psum | solution.py:44
  1930.2 81.7 %copy-start.7 = (f32[128,512]{1,0:T(8,128)S(1)}, f32[128,512]{1,0:T(8,128)}, u32[]{:S(2)}) copy-start(f32[128,512]{1,0:T(8,128)} %copy-done.6) | copy-start | bytes 786436
Sparse Core Ops, SparseCore 0:
  9.2 74.0 all-gather.2
  86.8 83.7 all-reduce.16
  243.8 77.8 all-reduce.18
  327.0 87.6 all-reduce.20
  484.9 77.8 all-reduce.22
  568.7 87.6 all-reduce.24
  726.5 77.8 all-reduce.26
  809.7 87.5 all-reduce.28
  967.5 77.8 all-reduce.30
  1051.4 87.6 all-reduce.32
  1209.2 77.8 all-reduce.34
  1292.4 87.6 all-reduce.36
  1450.3 77.8 all-reduce.38
  1534.2 87.6 all-reduce.40
  1692.1 77.8 all-reduce.42
  1776.0 87.6 all-reduce.44
  1933.9 77.8 all-reduce.46
where the time goes:
time: 2030 us; the launch traced here: 2020 us
  waiting for transfers between devices  1440 us (71%)
  blocking collectives  451 us (22%)
  matrix products  53.4 us (3%)
  other arithmetic  38 us (2%)
    psum x8, waiting for transfers between devices, shards(): summed = lax.psum(product, 'prow')  698 us
    psum x8, waiting for transfers between devices, shards(): diagonal = lax.psum(local_term, 'prow')  614 us
    all_to_all x7, blocking collectives, shards(): lax.all_to_all(outgoing, 'pcol', split_axis=0, concat_axis=0, tiled=True)  451 us
    all_gather x1, waiting for transfers between devices, shards(): whole_row = lax.all_gather(local_factor, 'pcol', axis=0, tiled=True)  72.1 us
    all_to_all x1, waiting for transfers between devices, shards(): lax.all_to_all(outgoing, 'pcol', split_axis=0, concat_axis=0, tiled=True)  50.3 us
  transfers between devices with their start and end apart: 18, of which 18 were waited for; matrix products, arithmetic and copies ran while one was open for 1% of the time, Pallas kernels for 0%

commit v1 on v0

v1 whole, which is shorter than its diff:
```python
import jax
import jax.numpy as jnp
from jax import lax
from jax.experimental import pallas as pl
from jax.experimental.pallas import tpu as pltpu
from jax.sharding import PartitionSpec as P

MESH = pl.DeviceIdType.MESH
NODES = 8
WIDTH = 512
SHARES = 4
ROWS = 128
HALF = ROWS // 2
SUBS = 2
PIECE = HALF // SUBS
AHEAD, BEHIND = 4, 3


def pattern_weight(lists_ref, parent_ref, target, node):
    found = parent_ref[target] == node
    for i in range(NODES - 1):
        found = jnp.logical_or(found, lists_ref[target, i] == node)
    return jnp.where(found, 1.0, 0.0).astype(jnp.float32)


def split(value):
    high = value.astype(jnp.bfloat16)
    low = (value - high.astype(jnp.float32)).astype(jnp.bfloat16)
    return high, low


def product(left, high_ref, low_ref, transposed):
    high, low = split(left)
    dims = (((1,), (1 if transposed else 0,)), ((), ()))
    rows = left.shape[0]
    both = lax.dot_general(
        jnp.concatenate([high, low], 0), high_ref[...], dims, preferred_element_type=jnp.float32
    )
    cross = lax.dot_general(high, low_ref[...], dims, preferred_element_type=jnp.float32)
    return both[:rows] + both[rows:] + cross


def kernel(
    f_hbm, d_hbm, lists_hbm, parent_hbm, out_ref,
    f_ref, d_ref, lists_ref, parent_ref,
    raw, lhi, llo, dhi, dlo, mine, mrecv, zacc, psend, precv, xrecv, across, trecv,
    in_sem, z_send, z_recv, y_send, y_recv, c_send, c_recv,
    m_send, m_recv, p_send, p_recv, x_send, x_recv, a_send, a_recv, t_send, t_recv,
):
    node = lax.axis_index("prow")
    col = lax.axis_index("pcol")
    plane = col // SHARES
    share = lax.rem(col, SHARES)
    y_low, core = share // 2, lax.rem(share, 2)
    y_share = (1 - y_low) * 2 + core
    c_share = y_low * 2 + 1 - core
    upper = plane // (NODES // 2)
    mirror = NODES - 1 - plane
    blocks = (jnp.minimum(plane, mirror), jnp.maximum(plane, mirror))

    def device(n, z, s):
        return (n, z * SHARES + s)

    barrier = pltpu.get_barrier_semaphore()

    def greet(target):
        pl.semaphore_signal(barrier, device_id=target, device_id_type=MESH)

    for step in range(1, NODES):
        greet(device(lax.rem(node + step, NODES), plane, share))
    greet(device(node, lax.rem(plane + 1, NODES), share))
    greet(device(node, lax.rem(plane + NODES - 1, NODES), share))
    greet(device(node, mirror, share))
    greet(device(node, plane, y_share))
    greet(device(node, plane, c_share))

    @pl.when(node < plane)
    def _():
        for s in range(SHARES):
            greet(device(plane, plane, s))

    @pl.when(node == plane)
    def _():
        for step in range(1, NODES):
            greet(device(node, lax.rem(plane + step, NODES), share))


    loads = [
        pltpu.make_async_copy(src, dst, in_sem.at[i])
        for i, (src, dst) in enumerate(
            [(lists_hbm, lists_ref), (parent_hbm, parent_ref), (f_hbm, f_ref), (d_hbm, d_ref)]
        )
    ]
    for load in loads:
        load.start()
    for load in loads[:3]:
        load.wait()
    raw[plane, share] = f_ref[...] * pattern_weight(lists_ref, parent_ref, plane, node)
    for h in range(2):
        first = share * ROWS + upper * HALF
        rows = lax.broadcasted_iota(jnp.int32, (HALF, WIDTH), 0) + first
        columns = lax.broadcasted_iota(jnp.int32, (HALF, WIDTH), 1)
        unit = jnp.where(rows == columns, 1.0, 0.0).astype(jnp.float32)
        here = jnp.where(node == blocks[h], 1.0, 0.0).astype(jnp.float32)
        mrecv[blocks[h], h] = unit
        mine[h] = unit * here
    loads[3].wait()
    high, low = split(d_ref[...])
    dhi[...] = high
    dlo[...] = low
    greeted = NODES - 1 + 5 + jnp.where(node == plane, SHARES * node, 1)
    pl.semaphore_wait(barrier, greeted)

    def remote(src, dst, send, recv, target):
        return pltpu.make_async_remote_copy(
            src_ref=src, dst_ref=dst, send_sem=send, recv_sem=recv,
            device_id=target, device_id_type=MESH,
        )

    def z_copy(k, sub, way):
        step = 1 if way == 0 else NODES - 1
        here = raw.at[k, share, pl.ds(sub * HALF, HALF)]
        target = device(node, lax.rem(plane + step, NODES), share)
        return remote(here, here, z_send.at[k, sub, way], z_recv.at[k, sub], target)

    def y_copy(k, sub):
        here = raw.at[k, share, pl.ds(sub * HALF, HALF)]
        target = device(node, plane, y_share)
        return remote(here, here, y_send.at[k, sub], y_recv.at[k, sub], target)

    def c_copy(k, sub, which):
        here = raw.at[k, share if which == 0 else y_share, pl.ds(sub * HALF, HALF)]
        target = device(node, plane, c_share)
        return remote(here, here, c_send.at[k, sub, which], c_recv.at[k, sub, which], target)

    def part(ref, index, h, sub):
        if sub is None:
            return ref.at[index, h] if index is not None else ref.at[h]
        rows = pl.ds(sub * PIECE, PIECE)
        return ref.at[index, h, rows] if index is not None else ref.at[h, rows]

    def m_copy(k, target, h, sub):
        i = sub or 0
        return remote(
            part(mine, None, h, sub), part(mrecv, k, h, sub),
            m_send.at[target, h, i], m_recv.at[k, h, i], device(target, plane, share),
        )

    def p_copy(k, target, h, sub):
        i = sub or 0
        return remote(
            part(psend, target, h, sub), part(precv, k, h, sub),
            p_send.at[target, h, i], p_recv.at[k, h, i], device(target, plane, share),
        )

    def passes(k, way, distance):
        if distance > (BEHIND if way else AHEAD):
            return False
        if way == 0:
            return jnp.logical_and(k < node, k >= 2)
        return jnp.logical_and(k < node, jnp.logical_or(k >= 1, distance <= 1))

    def ring(distance):
        ways = [0, 1] if distance else [0]
        return [(way, lax.rem(plane + (distance if way else NODES - distance), NODES)) for way in ways]

    def each(distance, action):
        for way, k in ring(distance):
            if distance == 0 or passes(k, way, distance) is not False:
                @pl.when(jnp.logical_and(k < node, k >= blocks[0]))
                def _():
                    for sub in range(SUBS):
                        action(k, sub)

    def sends(distance, sub, action):
        for way, k in ring(distance):
            for onward in ([0, 1] if distance == 0 else [way]):
                further = passes(k, onward, distance + 1)
                if further is not False:
                    @pl.when(further)
                    def _():
                        action(k, sub, onward)

    def land(distance):
        for sub in range(SUBS):
            for way, k in ring(distance):
                arrives = passes(k, way, distance) if distance else False
                if arrives is not False:
                    @pl.when(arrives)
                    def _():
                        z_copy(k, sub, way).wait_recv()

            sends(distance, sub, lambda k, i, way: z_copy(k, i, way).start())
            for way, k in ring(distance):
                if distance == 0 or passes(k, way, distance) is not False:
                    @pl.when(jnp.logical_and(k < node, k >= blocks[0]))
                    def _():
                        y_copy(k, sub).start()
                        c_copy(k, sub, 0).start()

    def relay(k, sub):
        y_copy(k, sub).wait_recv()
        c_copy(k, sub, 1).start()

    def prepare(k, sub):
        c_copy(k, sub, 0).wait_recv()
        c_copy(k, sub, 1).wait_recv()
        for i in range(SHARES):
            high, low = split(raw[k, i, sub * HALF : (sub + 1) * HALF])
            rows = slice(i * ROWS + sub * HALF, i * ROWS + (sub + 1) * HALF)
            lhi[k, rows] = high
            llo[k, rows] = low

    for step in range(AHEAD + 3):
        if step <= AHEAD:
            land(step)
        if 1 <= step <= AHEAD + 1:
            each(step - 1, relay)
        if 2 <= step:
            each(step - 2, prepare)

    def forward(k, carry):
        for h in range(2):
            @pl.when(k >= blocks[h])
            def _():
                @pl.when(k > blocks[h])
                def _():
                    m_copy(k, node, h, None).wait_recv()

                mine[h] = mine[h] - product(mrecv[k, h], lhi.at[k], llo.at[k], True)

        return carry

    lax.fori_loop(0, node - 1, forward, 0)

    for h in range(2):
        @pl.when(node > blocks[h])
        def _():
            last = node - 1
            for sub in range(SUBS):
                @pl.when(last > blocks[h])
                def _():
                    m_copy(last, node, h, sub).wait_recv()

                rows = slice(sub * PIECE, (sub + 1) * PIECE)
                mine[h, rows] = mine[h, rows] - product(
                    mrecv[last, h, rows], lhi.at[last], llo.at[last], True
                )

                @pl.when(node < NODES - 1)
                def _():
                    m_copy(node, node + 1, h, sub).start()

            def body(target, carry):
                m_copy(node, target, h, None).start()
                return carry

            lax.fori_loop(node + 2, NODES, body, 0)

    for h in range(2):
        zacc[h] = product(mine[h], dhi, dlo, False)

    def collect(k, h, sub):
        p_copy(k, node, h, sub).wait_recv()
        rows = slice(0, HALF) if sub is None else slice(sub * PIECE, (sub + 1) * PIECE)
        zacc[h, rows] = zacc[h, rows] - precv[k, h, rows]

    def spread(to, h, sub):
        rows = slice(0, HALF) if sub is None else slice(sub * PIECE, (sub + 1) * PIECE)
        psend[to, h, rows] = product(zacc[h, rows], lhi.at[to], llo.at[to], False)
        p_copy(node, to, h, sub).start()

    for h in (1, 0):
        @pl.when(node >= blocks[h])
        def _():
            def backward(i, carry):
                collect(NODES - 1 - i, h, None)
                return carry

            lax.fori_loop(0, NODES - 2 - node, backward, 0)
            for sub in range(SUBS):
                @pl.when(node < NODES - 1)
                def _():
                    collect(node + 1, h, sub)

                @pl.when(node > blocks[h])
                def _():
                    spread(node - 1, h, sub)

    for h in (0, 1):
        def remaining(i, carry):
            spread(node - 2 - i, h, None)
            return carry

        lax.fori_loop(0, node - 1 - blocks[h], remaining, 0)

    for h in range(2):
        weight = pattern_weight(lists_ref, parent_ref, blocks[h], node)
        zacc[h] = zacc[h] * jnp.where(node == blocks[h], 1.0, weight)

    kept, sent = upper, 1 - upper

    def x_copy():
        target = device(node, mirror, share)
        return remote(zacc.at[sent], xrecv, x_send, x_recv, target)

    def a_copy(h):
        target = device(node, node, share)
        return remote(zacc.at[h], across.at[blocks[h], upper], a_send.at[h], a_recv.at[blocks[h], upper], target)

    def t_copy(k, half, s):
        columns = pl.ds(s * ROWS, ROWS)
        return remote(
            across.at[k, half, slice(None), columns], trecv.at[share, half],
            t_send.at[k, half, s], t_recv.at[share, half], device(k, plane, s),
        )

    def arrival(s, half):
        tile = trecv.at[s, half]
        return remote(tile, tile, t_send.at[0, 0, 0], t_recv.at[s, half], device(plane, plane, s))

    @pl.when(node >= mirror)
    def _():
        x_copy().start()

    for h in range(2):
        @pl.when(jnp.logical_and(node > blocks[h], node != plane))
        def _():
            a_copy(h).start()

        @pl.when(jnp.logical_and(node > blocks[h], node == plane))
        def _():
            across[blocks[h], upper] = zacc[h]

    @pl.when(node >= plane)
    def _():
        out_ref[pl.ds(upper * HALF, HALF)] = zacc[kept]
        x_copy().wait_recv()
        out_ref[pl.ds((1 - upper) * HALF, HALF)] = xrecv[...]

    @pl.when(node == plane)
    def _():
        def deal(i, carry):
            k = node - 1 - i
            for half in range(2):
                source = jnp.minimum(k, NODES - 1 - k) if half == 0 else jnp.maximum(k, NODES - 1 - k)

                @pl.when(source != plane)
                def _():
                    into = across.at[k, half]
                    remote(into, into, a_send.at[0], a_recv.at[k, half], device(node, source, share)).wait_recv()

                for s in range(SHARES):
                    t_copy(k, half, s).start()
            return carry

        lax.fori_loop(0, node, deal, 0)

    @pl.when(node < plane)
    def _():
        for s in range(SHARES):
            for half in range(2):
                arrival(s, half).wait_recv()
        for s in range(SHARES):
            tiles = jnp.concatenate([trecv[s, 0], trecv[s, 1]], 0)
            out_ref[:, s * ROWS : (s + 1) * ROWS] = tiles.T

    @pl.when(node >= mirror)
    def _():
        x_copy().wait_send()

    @pl.when(node == plane)
    def _():
        def drain_t(k, carry):
            for half in range(2):
                for s in range(SHARES):
                    t_copy(k, half, s).wait_send()
            return carry

        lax.fori_loop(0, node, drain_t, 0)

    for distance in range(AHEAD + 1):
        def drained(k, sub):
            y_copy(k, sub).wait_send()
            c_copy(k, sub, 0).wait_send()
            c_copy(k, sub, 1).wait_send()

        each(distance, drained)
        for sub in range(SUBS):
            sends(distance, sub, lambda k, i, way: z_copy(k, i, way).wait_send())

    for h in range(2):
        @pl.when(node > blocks[h])
        def _():
            @pl.when(node != plane)
            def _():
                a_copy(h).wait_send()

            for sub in range(SUBS):
                p_copy(node, node - 1, h, sub).wait_send()

                @pl.when(node < NODES - 1)
                def _():
                    m_copy(node, node + 1, h, sub).wait_send()

        def drain_m(target, carry):
            m_copy(node, target, h, None).wait_send()
            return carry

        def drain_p(target, carry):
            p_copy(node, target, h, None).wait_send()
            return carry

        lax.fori_loop(node + 2, jnp.where(node > blocks[h], NODES, 0), drain_m, 0)
        lax.fori_loop(blocks[h], node - 1, drain_p, 0)


def shards(factor_panels, diag_inverse, block_lists, parent):
    f32, bf16, i32 = jnp.float32, jnp.bfloat16, jnp.int32
    dma = pltpu.SemaphoreType.DMA
    anywhere = pl.BlockSpec(memory_space=pl.ANY)
    messages = pltpu.VMEM((NODES, 2, HALF, WIDTH), f32)
    pair = pltpu.VMEM((2, HALF, WIDTH), f32)
    half = pltpu.VMEM((HALF, WIDTH), f32)
    row = pltpu.VMEM((NODES, WIDTH, WIDTH), bf16)
    block = pltpu.VMEM((WIDTH, WIDTH), bf16)
    flags = dma((NODES, 2, 2))
    inverse = pl.pallas_call(
        kernel,
        out_shape=jax.ShapeDtypeStruct((ROWS, WIDTH), f32),
        in_specs=[anywhere] * 4,
        out_specs=pl.BlockSpec(memory_space=pltpu.VMEM),
        scratch_shapes=[
            pltpu.VMEM((ROWS, WIDTH), f32), pltpu.VMEM((WIDTH, WIDTH), f32),
            pltpu.SMEM((NODES, NODES - 1), i32), pltpu.SMEM((NODES,), i32),
            pltpu.VMEM((NODES, SHARES, ROWS, WIDTH), f32),
            row, row, block, block, pair, messages, pair, messages, messages, half,
            messages, pltpu.VMEM((SHARES, 2, HALF, ROWS), f32),
            dma((4,)), flags, dma((NODES, SUBS)), dma((NODES, SUBS)), dma((NODES, SUBS)),
            flags, flags,
            flags, flags, flags, flags, dma(()), dma(()), dma((2,)), dma((NODES, 2)),
            dma((NODES, 2, SHARES)), dma((SHARES, 2)),
        ],
        compiler_params=pltpu.CompilerParams(
            collective_id=0, has_side_effects=True, vmem_limit_bytes=60 * 2**20
        ),
        name="selected_inverse",
    )(factor_panels[0], diag_inverse[0], block_lists, parent)
    return inverse[None]


def solution(mesh):
    placed = (P("prow", "pcol", None), P("prow", None, None), P(), P())
    return jax.shard_map(
        shards, mesh=mesh, in_specs=placed, out_specs=P("prow", "pcol", None), check_vma=False
    )
```

time: 2030 us -> 110 us (0.05)
  waiting for transfers between devices: 1440 us -> 0 us
  blocking collectives: 451 us -> 0 us
  Pallas kernels: 0 us -> 108 us
  matrix products: 53.4 us -> 0 us
  other arithmetic: 38 us -> 0 us
    psum x16 -> x0, waiting for transfers between devices: 1310 us -> none  [the longest x8 698 us: shards(): summed = lax.psum(product, 'prow')]
    all_to_all x7 -> x0, blocking collectives: 451 us -> none  [shards(): lax.all_to_all(outgoing, 'pcol', split_axis=0, concat_axis=0, tiled=True)]
    pallas_call x0 -> x1, Pallas kernels: none -> 108 us  [shards(): pl.pallas_call(kernel, out_shape=jax.ShapeDtypeStruct((ROWS, WIDTH), f32)...]
    all_gather x1 -> x0, waiting for transfers between devices: 72.1 us -> none  [shards(): whole_row = lax.all_gather(local_factor, 'pcol', axis=0, tiled=True)]
    dot_general x16 -> x0, matrix products: 53.4 us -> none  [the longest x8 26.7 us: shards(): local_term = jnp.dot(mirror_rows, panel, precision=lax.Precision.HIGHEST)]
    all_to_all x1 -> x0, waiting for transfers between devices: 50.3 us -> none  [shards(): lax.all_to_all(outgoing, 'pcol', split_axis=0, concat_axis=0, tiled=True)]
  transfers between devices with their start and end apart: 18 -> 0, of which waited for: 18 -> 0; matrix products, arithmetic and copies ran while one was open for 1% -> 0% of each run, Pallas kernels for 0% -> 0%
where the time goes in v1:
time: 110 us
  Pallas kernels  108 us (98%)
  local copies, waits for them, and re-layouts  1.67 us (2%)
    pallas_call x1, Pallas kernels, shards(): pl.pallas_call(kernel, out_shape=jax.ShapeDtypeStruct((ROWS, WIDTH), f32)...  108 us

profile of v1, /device:TPU:41, one launch (start us, length us, event | category | flops | bytes accessed | tf_op | source)
XLA Modules:
  0.0 109.7 jit_solution(9032964575504308912)
XLA Ops:
  0.0 108.0 %selected_inverse.1 = f32[128,512]{1,0:T(8,128)} custom-call(f32[128,512]{1,0:T(8,128)} %bitcast.5, f32[512,512]{1,0:T(8,128)} %bitcast.3, s32[8,7]{1,0:T(8,128)} %lists_hbm.1, s32[8]{0:T(128)} %parent_hbm.1), custom_call_target="tpu_custom_call" | custom-call | tf_op jit(solution)/shard_map/selected_inverse/pallas_call | solution.py:428
  108.0 1.7 %copy.6 = f32[1,128,512]{2,1,0:T(8,128)} copy(f32[1,128,512]{2,1,0:T(8,128)} %bitcast.4) | data formatting | bytes 524288

commit v2 on v1

--- a/solution.py
+++ b/solution.py
@@ -13,7 +13,10 @@
 HALF = ROWS // 2
 SUBS = 2
 PIECE = HALF // SUBS
+DIRECT = 3
 AHEAD, BEHIND = 4, 3
+KEPT = 5
+RELAY, PREPARE = 3, 4
 
 
 def pattern_weight(lists_ref, parent_ref, target, node):
@@ -44,7 +47,9 @@
     f_hbm, d_hbm, lists_hbm, parent_hbm, out_ref,
     f_ref, d_ref, lists_ref, parent_ref,
     raw, lhi, llo, dhi, dlo, mine, mrecv, zacc, psend, precv, xrecv, across, trecv,
+    scaled, part_sum, part_recv, solved,
     in_sem, z_send, z_recv, y_send, y_recv, c_send, c_recv,
+    h_send, h_recv, s_send, s_recv, v_send, v_recv,
     m_send, m_recv, p_send, p_recv, x_send, x_recv, a_send, a_recv, t_send, t_recv,
 ):
     node = lax.axis_index("prow")
@@ -57,6 +62,9 @@
     upper = plane // (NODES // 2)
     mirror = NODES - 1 - plane
     blocks = (jnp.minimum(plane, mirror), jnp.maximum(plane, mirror))
+    first = jnp.maximum(node - KEPT, 0)
+    friend = NODES - 1 - node
+    helped = NODES - 1 - KEPT - node
 
     def device(n, z, s):
         return (n, z * SHARES + s)
@@ -76,10 +84,18 @@
 
     @pl.when(node < plane)
     def _():
-        for s in range(SHARES):
-            greet(device(plane, plane, s))
-
-    @pl.when(node == plane)
+        @pl.when(plane > DIRECT)
+        def _():
+            for s in range(SHARES):
+                greet(device(plane, plane, s))
+
+        @pl.when(plane <= DIRECT)
+        def _():
+            for s in range(SHARES):
+                greet(device(plane, node, s))
+                greet(device(plane, NODES - 1 - node, s))
+
+    @pl.when(jnp.logical_and(node == plane, node > DIRECT))
     def _():
         for step in range(1, NODES):
             greet(device(node, lax.rem(plane + step, NODES), share))
@@ -95,20 +111,30 @@
         load.start()
     for load in loads[:3]:
         load.wait()
-    raw[plane, share] = f_ref[...] * pattern_weight(lists_ref, parent_ref, plane, node)
+
+    @pl.when(plane < node)
+    def _():
+        raw[plane, share] = f_ref[...] * pattern_weight(lists_ref, parent_ref, plane, node)
+
     for h in range(2):
-        first = share * ROWS + upper * HALF
-        rows = lax.broadcasted_iota(jnp.int32, (HALF, WIDTH), 0) + first
+        offset = share * ROWS + upper * HALF
+        rows = lax.broadcasted_iota(jnp.int32, (HALF, WIDTH), 0) + offset
         columns = lax.broadcasted_iota(jnp.int32, (HALF, WIDTH), 1)
         unit = jnp.where(rows == columns, 1.0, 0.0).astype(jnp.float32)
         here = jnp.where(node == blocks[h], 1.0, 0.0).astype(jnp.float32)
         mrecv[blocks[h], h] = unit
         mine[h] = unit * here
+    weights = []
+    for h in range(2):
+        weight = pattern_weight(lists_ref, parent_ref, blocks[h], node)
+        weights.append(jnp.where(node == blocks[h], 1.0, weight))
     loads[3].wait()
     high, low = split(d_ref[...])
     dhi[...] = high
     dlo[...] = low
-    greeted = NODES - 1 + 5 + jnp.where(node == plane, SHARES * node, 1)
+    relayed = jnp.where(node == plane, SHARES * node, 1)
+    direct = SHARES * sum(jnp.where(node > blocks[h], 1, 0) for h in range(2))
+    greeted = NODES - 1 + 5 + jnp.where(node > DIRECT, relayed, direct)
     pl.semaphore_wait(barrier, greeted)
 
     def remote(src, dst, send, recv, target):
@@ -153,71 +179,91 @@
             p_send.at[target, h, i], p_recv.at[k, h, i], device(target, plane, share),
         )
 
-    def passes(k, way, distance):
+    def member(k, kind):
+        return k < helped if kind else jnp.logical_and(k >= first, k < node)
+
+    def used(k, kind):
+        return jnp.logical_and(member(k, kind), k >= blocks[0])
+
+    def passes(k, way, distance, kind):
         if distance > (BEHIND if way else AHEAD):
             return False
         if way == 0:
-            return jnp.logical_and(k < node, k >= 2)
-        return jnp.logical_and(k < node, jnp.logical_or(k >= 1, distance <= 1))
+            return jnp.logical_and(member(k, kind), k >= 2)
+        return jnp.logical_and(member(k, kind), jnp.logical_or(k >= 1, distance <= 1))
 
     def ring(distance):
         ways = [0, 1] if distance else [0]
         return [(way, lax.rem(plane + (distance if way else NODES - distance), NODES)) for way in ways]
 
-    def each(distance, action):
+    def each(distance, kind, action):
         for way, k in ring(distance):
-            if distance == 0 or passes(k, way, distance) is not False:
-                @pl.when(jnp.logical_and(k < node, k >= blocks[0]))
+            if distance == 0 or passes(k, way, distance, kind) is not False:
+                @pl.when(used(k, kind))
                 def _():
                     for sub in range(SUBS):
-                        action(k, sub)
-
-    def sends(distance, sub, action):
+                        action(k, k + KEPT * kind, sub)
+
+    def sends(distance, sub, kind, action):
         for way, k in ring(distance):
             for onward in ([0, 1] if distance == 0 else [way]):
-                further = passes(k, onward, distance + 1)
+                further = passes(k, onward, distance + 1, kind)
                 if further is not False:
                     @pl.when(further)
                     def _():
-                        action(k, sub, onward)
-
-    def land(distance):
+                        action(k, k + KEPT * kind, sub, onward)
+
+    def land(distance, kind):
         for sub in range(SUBS):
             for way, k in ring(distance):
-                arrives = passes(k, way, distance) if distance else False
+                arrives = passes(k, way, distance, kind) if distance else False
                 if arrives is not False:
                     @pl.when(arrives)
                     def _():
-                        z_copy(k, sub, way).wait_recv()
-
-            sends(distance, sub, lambda k, i, way: z_copy(k, i, way).start())
+                        z_copy(k + KEPT * kind, sub, way).wait_recv()
+
+            sends(distance, sub, kind, lambda k, slot, i, way: z_copy(slot, i, way).start())
             for way, k in ring(distance):
-                if distance == 0 or passes(k, way, distance) is not False:
-                    @pl.when(jnp.logical_and(k < node, k >= blocks[0]))
+                if distance == 0 or passes(k, way, distance, kind) is not False:
+                    @pl.when(used(k, kind))
                     def _():
-                        y_copy(k, sub).start()
-                        c_copy(k, sub, 0).start()
-
-    def relay(k, sub):
-        y_copy(k, sub).wait_recv()
-        c_copy(k, sub, 1).start()
-
-    def prepare(k, sub):
-        c_copy(k, sub, 0).wait_recv()
-        c_copy(k, sub, 1).wait_recv()
+                        y_copy(k + KEPT * kind, sub).start()
+                        c_copy(k + KEPT * kind, sub, 0).start()
+
+    def relay(distance, kind):
+        def action(k, slot, sub):
+            y_copy(slot, sub).wait_recv()
+            c_copy(slot, sub, 1).start()
+
+        each(distance, kind, action)
+
+    def prepare(k, slot, sub):
+        c_copy(slot, sub, 0).wait_recv()
+        c_copy(slot, sub, 1).wait_recv()
         for i in range(SHARES):
-            high, low = split(raw[k, i, sub * HALF : (sub + 1) * HALF])
+            high, low = split(raw[slot, i, sub * HALF : (sub + 1) * HALF])
             rows = slice(i * ROWS + sub * HALF, i * ROWS + (sub + 1) * HALF)
-            lhi[k, rows] = high
-            llo[k, rows] = low
-
-    for step in range(AHEAD + 3):
-        if step <= AHEAD:
-            land(step)
-        if 1 <= step <= AHEAD + 1:
-            each(step - 1, relay)
-        if 2 <= step:
-            each(step - 2, prepare)
+            lhi[slot, rows] = high
+            llo[slot, rows] = low
+
+    def gather(kind):
+        for step in range(AHEAD + 1 + PREPARE):
+            if step <= AHEAD:
+                land(step, kind)
+            if 0 <= step - RELAY <= AHEAD:
+                relay(step - RELAY, kind)
+            if 0 <= step - PREPARE <= AHEAD:
+                each(step - PREPARE, kind, prepare)
+
+    def hand_over():
+        target = device(friend, plane, share)
+        return remote(raw.at[plane, share], raw.at[plane + KEPT, share], h_send, h_recv, target)
+
+    @pl.when(plane < first)
+    def _():
+        hand_over().start()
+
+    gather(0)
 
     def forward(k, carry):
         for h in range(2):
@@ -231,7 +277,15 @@
 
         return carry
 
-    lax.fori_loop(0, node - 1, forward, 0)
+    lax.fori_loop(first, node - 1, forward, 0)
+
+    def s_copy():
+        return remote(part_sum, part_recv, s_send, s_recv, device(friend, plane, share))
+
+    @pl.when(blocks[0] < first)
+    def _():
+        s_copy().wait_recv()
+        mine[0] = mine[0] - part_recv[...]
 
     for h in range(2):
         @pl.when(node > blocks[h])
@@ -255,13 +309,72 @@
                 m_copy(node, target, h, None).start()
                 return carry
 
-            lax.fori_loop(node + 2, NODES, body, 0)
+            lax.fori_loop(node + 2, jnp.minimum(node + KEPT + 1, NODES), body, 0)
+
+    @pl.when(jnp.logical_and(node > blocks[0], jnp.logical_and(node >= 1, node <= NODES - 2 - KEPT)))
+    def _():
+        m_copy(node, 0, 0, None).start()
+        mrecv[node, 0] = mine[0]
+
+    @pl.when(plane < helped)
+    def _():
+        remote(raw.at[0, 0], raw.at[0, 0], h_send, h_recv, device(friend, plane, share)).wait_recv()
+
+    gather(1)
+
+    @pl.when(blocks[0] < helped)
+    def _():
+        part_sum[...] = jnp.zeros_like(part_sum)
+
+        def term(k, carry):
+            @pl.when(jnp.logical_and(k > blocks[0], k != node))
+            def _():
+                m_copy(k, node, 0, None).wait_recv()
+
+            part_sum[...] += product(mrecv[k, 0], lhi.at[k + KEPT], llo.at[k + KEPT], True)
+            return carry
+
+        lax.fori_loop(blocks[0], helped, term, 0)
+        s_copy().start()
 
     for h in range(2):
         zacc[h] = product(mine[h], dhi, dlo, False)
 
+    def v_copy():
+        return remote(zacc.at[0], solved, v_send, v_recv, device(friend, plane, share))
+
+    def early_copy(to):
+        return remote(
+            psend.at[to + KEPT, 0], precv.at[friend, 0],
+            p_send.at[to + KEPT, 0, 0], p_recv.at[friend, 0, 0], device(to, plane, share),
+        )
+
+    @pl.when(blocks[0] < helped)
+    def _():
+        v_copy().wait_recv()
+
+        def early(to, carry):
+            psend[to + KEPT, 0] = product(solved[...], lhi.at[to + KEPT], llo.at[to + KEPT], False)
+
+            @pl.when(to != node)
+            def _():
+                early_copy(to).start()
+
+            @pl.when(to == node)
+            def _():
+                precv[friend, 0] = psend[to + KEPT, 0]
+
+            return carry
+
+        lax.fori_loop(blocks[0], helped, early, 0)
+
     def collect(k, h, sub):
-        p_copy(k, node, h, sub).wait_recv()
+        if h == 0 and sub is None:
+            @pl.when(jnp.logical_not(jnp.logical_and(k == friend, node < helped)))
+            def _():
+                p_copy(k, node, h, sub).wait_recv()
+        else:
+            p_copy(k, node, h, sub).wait_recv()
         rows = slice(0, HALF) if sub is None else slice(sub * PIECE, (sub + 1) * PIECE)
         zacc[h, rows] = zacc[h, rows] - precv[k, h, rows]
 
@@ -287,26 +400,29 @@
                 def _():
                     spread(node - 1, h, sub)
 
+    @pl.when(blocks[0] < first)
+    def _():
+        v_copy().start()
+
     for h in (0, 1):
         def remaining(i, carry):
             spread(node - 2 - i, h, None)
             return carry
 
-        lax.fori_loop(0, node - 1 - blocks[h], remaining, 0)
+        lax.fori_loop(0, node - 1 - jnp.maximum(blocks[h], first), remaining, 0)
 
     for h in range(2):
-        weight = pattern_weight(lists_ref, parent_ref, blocks[h], node)
-        zacc[h] = zacc[h] * jnp.where(node == blocks[h], 1.0, weight)
+        scaled[h] = zacc[h] * weights[h]
 
     kept, sent = upper, 1 - upper
 
     def x_copy():
         target = device(node, mirror, share)
-        return remote(zacc.at[sent], xrecv, x_send, x_recv, target)
+        return remote(scaled.at[sent], xrecv, x_send, x_recv, target)
 
     def a_copy(h):
         target = device(node, node, share)
-        return remote(zacc.at[h], across.at[blocks[h], upper], a_send.at[h], a_recv.at[blocks[h], upper], target)
+        return remote(scaled.at[h], across.at[blocks[h], upper], a_send.at[h], a_recv.at[blocks[h], upper], target)
 
     def t_copy(k, half, s):
         columns = pl.ds(s * ROWS, ROWS)
@@ -315,6 +431,12 @@
             t_send.at[k, half, s], t_recv.at[share, half], device(k, plane, s),
         )
 
+    def d_copy(h, s):
+        return remote(
+            scaled.at[h, slice(None), pl.ds(s * ROWS, ROWS)], trecv.at[share, upper],
+            t_send.at[blocks[h], upper, s], t_recv.at[share, upper], device(blocks[h], node, s),
+        )
+
     def arrival(s, half):
         tile = trecv.at[s, half]
         return remote(tile, tile, t_send.at[0, 0, 0], t_recv.at[s, half], device(plane, plane, s))
@@ -324,21 +446,26 @@
         x_copy().start()
 
     for h in range(2):
-        @pl.when(jnp.logical_and(node > blocks[h], node != plane))
+        @pl.when(jnp.logical_and(node > blocks[h], node <= DIRECT))
+        def _():
+            for s in range(SHARES):
+                d_copy(h, s).start()
+
+        @pl.when(jnp.logical_and(node > jnp.maximum(blocks[h], DIRECT), node != plane))
         def _():
             a_copy(h).start()
 
-        @pl.when(jnp.logical_and(node > blocks[h], node == plane))
-        def _():
-            across[blocks[h], upper] = zacc[h]
+        @pl.when(jnp.logical_and(node > jnp.maximum(blocks[h], DIRECT), node == plane))
+        def _():
+            across[blocks[h], upper] = scaled[h]
 
     @pl.when(node >= plane)
     def _():
-        out_ref[pl.ds(upper * HALF, HALF)] = zacc[kept]
+        out_ref[pl.ds(upper * HALF, HALF)] = scaled[kept]
         x_copy().wait_recv()
         out_ref[pl.ds((1 - upper) * HALF, HALF)] = xrecv[...]
 
-    @pl.when(node == plane)
+    @pl.when(jnp.logical_and(node == plane, node > DIRECT))
     def _():
         def deal(i, carry):
             k = node - 1 - i
@@ -361,7 +488,6 @@
         for s in range(SHARES):
             for half in range(2):
                 arrival(s, half).wait_recv()
-        for s in range(SHARES):
             tiles = jnp.concatenate([trecv[s, 0], trecv[s, 1]], 0)
             out_ref[:, s * ROWS : (s + 1) * ROWS] = tiles.T
 
@@ -369,7 +495,7 @@
     def _():
         x_copy().wait_send()
 
-    @pl.when(node == plane)
+    @pl.when(jnp.logical_and(node == plane, node > DIRECT))
     def _():
         def drain_t(k, carry):
             for half in range(2):
@@ -379,22 +505,53 @@
 
         lax.fori_loop(0, node, drain_t, 0)
 
-    for distance in range(AHEAD + 1):
-        def drained(k, sub):
-            y_copy(k, sub).wait_send()
-            c_copy(k, sub, 0).wait_send()
-            c_copy(k, sub, 1).wait_send()
-
-        each(distance, drained)
-        for sub in range(SUBS):
-            sends(distance, sub, lambda k, i, way: z_copy(k, i, way).wait_send())
+    for kind in range(2):
+        for distance in range(AHEAD + 1):
+            def drained(k, slot, sub):
+                y_copy(slot, sub).wait_send()
+                c_copy(slot, sub, 0).wait_send()
+                c_copy(slot, sub, 1).wait_send()
+
+            each(distance, kind, drained)
+            for sub in range(SUBS):
+                sends(distance, sub, kind, lambda k, slot, i, way: z_copy(slot, i, way).wait_send())
+
+    @pl.when(plane < first)
+    def _():
+        hand_over().wait_send()
+
+    @pl.when(blocks[0] < first)
+    def _():
+        v_copy().wait_send()
+
+    @pl.when(jnp.logical_and(node > blocks[0], jnp.logical_and(node >= 1, node <= NODES - 2 - KEPT)))
+    def _():
+        m_copy(node, 0, 0, None).wait_send()
+
+    @pl.when(blocks[0] < helped)
+    def _():
+        s_copy().wait_send()
+
+        def drain_early(to, carry):
+            @pl.when(to != node)
+            def _():
+                early_copy(to).wait_send()
+
+            return carry
+
+        lax.fori_loop(blocks[0], helped, drain_early, 0)
 
     for h in range(2):
         @pl.when(node > blocks[h])
         def _():
-            @pl.when(node != plane)
+            @pl.when(jnp.logical_and(node != plane, node > DIRECT))
             def _():
                 a_copy(h).wait_send()
+
+            @pl.when(node <= DIRECT)
+            def _():
+                for s in range(SHARES):
+                    d_copy(h, s).wait_send()
 
             for sub in range(SUBS):
                 p_copy(node, node - 1, h, sub).wait_send()
@@ -411,8 +568,9 @@
             p_copy(node, target, h, None).wait_send()
             return carry
 
-        lax.fori_loop(node + 2, jnp.where(node > blocks[h], NODES, 0), drain_m, 0)
-        lax.fori_loop(blocks[h], node - 1, drain_p, 0)
+        reach = jnp.minimum(node + KEPT + 1, NODES)
+        lax.fori_loop(node + 2, jnp.where(node > blocks[h], reach, 0), drain_m, 0)
+        lax.fori_loop(jnp.maximum(blocks[h], first), node - 1, drain_p, 0)
 
 
 def shards(factor_panels, diag_inverse, block_lists, parent):
@@ -436,8 +594,9 @@
             pltpu.VMEM((NODES, SHARES, ROWS, WIDTH), f32),
             row, row, block, block, pair, messages, pair, messages, messages, half,
             messages, pltpu.VMEM((SHARES, 2, HALF, ROWS), f32),
+            pair, half, half, half,
             dma((4,)), flags, dma((NODES, SUBS)), dma((NODES, SUBS)), dma((NODES, SUBS)),
-            flags, flags,
+            flags, flags, *[dma(())] * 6,
             flags, flags, flags, flags, dma(()), dma(()), dma((2,)), dma((NODES, 2)),
             dma((NODES, 2, SHARES)), dma((SHARES, 2)),
         ],

time: 110 us -> 102 us (0.927)
  Pallas kernels: 108 us -> 99.2 us
    pallas_call x1, Pallas kernels: 108 us -> 99.2 us  [shards(): pl.pallas_call(kernel, out_shape=jax.ShapeDtypeStruct((ROWS, WIDTH), f32)...]
where the time goes in v2:
time: 102 us; the launch traced here: 101 us
  Pallas kernels  99.2 us (97%)
  local copies, waits for them, and re-layouts  1.67 us (2%)
    pallas_call x1, Pallas kernels, shards(): pl.pallas_call(kernel, out_shape=jax.ShapeDtypeStruct((ROWS, WIDTH), f32)...  99.2 us

profile of v2, /device:TPU:41, one launch (start us, length us, event | category | flops | bytes accessed | tf_op | source)
XLA Modules:
  0.0 100.9 jit_solution(4122191223431442203)
XLA Ops:
  0.0 99.2 %selected_inverse.1 = f32[128,512]{1,0:T(8,128)} custom-call(f32[128,512]{1,0:T(8,128)} %bitcast.5, f32[512,512]{1,0:T(8,128)} %bitcast.3, s32[8,7]{1,0:T(8,128)} %lists_hbm.1, s32[8]{0:T(128)} %parent_hbm.1), custom_call_target="tpu_custom_call" | custom-call | tf_op jit(solution)/shard_map/selected_inverse/pallas_call | solution.py:586
  99.2 1.7 %copy.6 = f32[1,128,512]{2,1,0:T(8,128)} copy(f32[1,128,512]{2,1,0:T(8,128)} %bitcast.4) | data formatting | bytes 524288

commit v3 on v2

--- a/solution.py
+++ b/solution.py
@@ -12,11 +12,12 @@
 ROWS = 128
 HALF = ROWS // 2
 SUBS = 2
+CUTS = 2
 PIECE = HALF // SUBS
 DIRECT = 3
 AHEAD, BEHIND = 4, 3
 KEPT = 5
-RELAY, PREPARE = 3, 4
+RELAY, PREPARE = 1, 2
 
 
 def pattern_weight(lists_ref, parent_ref, target, node):
@@ -201,7 +202,7 @@
             if distance == 0 or passes(k, way, distance, kind) is not False:
                 @pl.when(used(k, kind))
                 def _():
-                    for sub in range(SUBS):
+                    for sub in range(CUTS):
                         action(k, k + KEPT * kind, sub)
 
     def sends(distance, sub, kind, action):
@@ -214,7 +215,7 @@
                         action(k, k + KEPT * kind, sub, onward)
 
     def land(distance, kind):
-        for sub in range(SUBS):
+        for sub in range(CUTS):
             for way, k in ring(distance):
                 arrives = passes(k, way, distance, kind) if distance else False
                 if arrives is not False:
@@ -337,9 +338,6 @@
         lax.fori_loop(blocks[0], helped, term, 0)
         s_copy().start()
 
-    for h in range(2):
-        zacc[h] = product(mine[h], dhi, dlo, False)
-
     def v_copy():
         return remote(zacc.at[0], solved, v_send, v_recv, device(friend, plane, share))
 
@@ -383,9 +381,11 @@
         psend[to, h, rows] = product(zacc[h, rows], lhi.at[to], llo.at[to], False)
         p_copy(node, to, h, sub).start()
 
-    for h in (1, 0):
+    for h in (0, 1):
         @pl.when(node >= blocks[h])
         def _():
+            zacc[h] = product(mine[h], dhi, dlo, False)
+
             def backward(i, carry):
                 collect(NODES - 1 - i, h, None)
                 return carry
@@ -412,7 +412,7 @@
         lax.fori_loop(0, node - 1 - jnp.maximum(blocks[h], first), remaining, 0)
 
     for h in range(2):
-        scaled[h] = zacc[h] * weights[h]
+        scaled[h] = jnp.where(weights[h] > 0.0, zacc[h], 0.0)
 
     kept, sent = upper, 1 - upper
 
@@ -513,7 +513,7 @@
                 c_copy(slot, sub, 1).wait_send()
 
             each(distance, kind, drained)
-            for sub in range(SUBS):
+            for sub in range(CUTS):
                 sends(distance, sub, kind, lambda k, slot, i, way: z_copy(slot, i, way).wait_send())
 
     @pl.when(plane < first)
@@ -582,7 +582,8 @@
     half = pltpu.VMEM((HALF, WIDTH), f32)
     row = pltpu.VMEM((NODES, WIDTH, WIDTH), bf16)
     block = pltpu.VMEM((WIDTH, WIDTH), bf16)
-    flags = dma((NODES, 2, 2))
+    flags = dma((NODES, 2, SUBS))
+    row_cuts, cuts = dma((NODES, CUTS)), dma((NODES, CUTS, 2))
     inverse = pl.pallas_call(
         kernel,
         out_shape=jax.ShapeDtypeStruct((ROWS, WIDTH), f32),
@@ -595,8 +596,7 @@
             row, row, block, block, pair, messages, pair, messages, messages, half,
             messages, pltpu.VMEM((SHARES, 2, HALF, ROWS), f32),
             pair, half, half, half,
-            dma((4,)), flags, dma((NODES, SUBS)), dma((NODES, SUBS)), dma((NODES, SUBS)),
-            flags, flags, *[dma(())] * 6,
+            dma((4,)), cuts, row_cuts, row_cuts, row_cuts, cuts, cuts, *[dma(())] * 6,
             flags, flags, flags, flags, dma(()), dma(()), dma((2,)), dma((NODES, 2)),
             dma((NODES, 2, SHARES)), dma((SHARES, 2)),
         ],

time: 102 us -> 102 us (level)
  no operation moved by 1% of the time
where the time goes in v3:
time: 102 us
  Pallas kernels  99.8 us (98%)
  local copies, waits for them, and re-layouts  1.67 us (2%)
    pallas_call x1, Pallas kernels, shards(): pl.pallas_call(kernel, out_shape=jax.ShapeDtypeStruct((ROWS, WIDTH), f32)...  99.8 us

profile of v3, /device:TPU:41, one launch (start us, length us, event | category | flops | bytes accessed | tf_op | source)
XLA Modules:
  0.0 101.5 jit_solution(2497662381190122688)
XLA Ops:
  0.0 99.8 %selected_inverse.1 = f32[128,512]{1,0:T(8,128)} custom-call(f32[128,512]{1,0:T(8,128)} %bitcast.5, f32[512,512]{1,0:T(8,128)} %bitcast.3, s32[8,7]{1,0:T(8,128)} %lists_hbm.1, s32[8]{0:T(128)} %parent_hbm.1), custom_call_target="tpu_custom_call" | custom-call | tf_op jit(solution)/shard_map/selected_inverse/pallas_call | solution.py:587
  99.8 1.7 %copy.6 = f32[1,128,512]{2,1,0:T(8,128)} copy(f32[1,128,512]{2,1,0:T(8,128)} %bitcast.4) | data formatting | bytes 524288

commit v4 on v3

--- a/solution.py
+++ b/solution.py
@@ -102,6 +102,10 @@
             greet(device(node, lax.rem(plane + step, NODES), share))
 
 
+    @pl.when(plane < helped)
+    def _():
+        greet(device(friend, plane, y_share))
+
     loads = [
         pltpu.make_async_copy(src, dst, in_sem.at[i])
         for i, (src, dst) in enumerate(
@@ -135,7 +139,7 @@
     dlo[...] = low
     relayed = jnp.where(node == plane, SHARES * node, 1)
     direct = SHARES * sum(jnp.where(node > blocks[h], 1, 0) for h in range(2))
-    greeted = NODES - 1 + 5 + jnp.where(node > DIRECT, relayed, direct)
+    greeted = NODES - 1 + 5 + jnp.where(node > DIRECT, relayed, direct) + jnp.where(plane < first, 1, 0)
     pl.semaphore_wait(barrier, greeted)
 
     def remote(src, dst, send, recv, target):
@@ -144,19 +148,19 @@
             device_id=target, device_id_type=MESH,
         )
 
-    def z_copy(k, sub, way):
+    def z_copy(k, sub, way, kind):
         step = 1 if way == 0 else NODES - 1
-        here = raw.at[k, share, pl.ds(sub * HALF, HALF)]
+        here = raw.at[k, y_share if kind else share, pl.ds(sub * HALF, HALF)]
         target = device(node, lax.rem(plane + step, NODES), share)
         return remote(here, here, z_send.at[k, sub, way], z_recv.at[k, sub], target)
 
-    def y_copy(k, sub):
-        here = raw.at[k, share, pl.ds(sub * HALF, HALF)]
+    def y_copy(k, sub, kind):
+        here = raw.at[k, y_share if kind else share, pl.ds(sub * HALF, HALF)]
         target = device(node, plane, y_share)
         return remote(here, here, y_send.at[k, sub], y_recv.at[k, sub], target)
 
-    def c_copy(k, sub, which):
-        here = raw.at[k, share if which == 0 else y_share, pl.ds(sub * HALF, HALF)]
+    def c_copy(k, sub, which, kind):
+        here = raw.at[k, share if which == kind else y_share, pl.ds(sub * HALF, HALF)]
         target = device(node, plane, c_share)
         return remote(here, here, c_send.at[k, sub, which], c_recv.at[k, sub, which], target)
 
@@ -221,26 +225,26 @@
                 if arrives is not False:
                     @pl.when(arrives)
                     def _():
-                        z_copy(k + KEPT * kind, sub, way).wait_recv()
-
-            sends(distance, sub, kind, lambda k, slot, i, way: z_copy(slot, i, way).start())
+                        z_copy(k + KEPT * kind, sub, way, kind).wait_recv()
+
+            sends(distance, sub, kind, lambda k, slot, i, way: z_copy(slot, i, way, kind).start())
             for way, k in ring(distance):
                 if distance == 0 or passes(k, way, distance, kind) is not False:
                     @pl.when(used(k, kind))
                     def _():
-                        y_copy(k + KEPT * kind, sub).start()
-                        c_copy(k + KEPT * kind, sub, 0).start()
+                        y_copy(k + KEPT * kind, sub, kind).start()
+                        c_copy(k + KEPT * kind, sub, 0, kind).start()
 
     def relay(distance, kind):
         def action(k, slot, sub):
-            y_copy(slot, sub).wait_recv()
-            c_copy(slot, sub, 1).start()
+            y_copy(slot, sub, kind).wait_recv()
+            c_copy(slot, sub, 1, kind).start()
 
         each(distance, kind, action)
 
-    def prepare(k, slot, sub):
-        c_copy(slot, sub, 0).wait_recv()
-        c_copy(slot, sub, 1).wait_recv()
+    def prepare(k, slot, sub, kind):
+        c_copy(slot, sub, 0, kind).wait_recv()
+        c_copy(slot, sub, 1, kind).wait_recv()
         for i in range(SHARES):
             high, low = split(raw[slot, i, sub * HALF : (sub + 1) * HALF])
             rows = slice(i * ROWS + sub * HALF, i * ROWS + (sub + 1) * HALF)
@@ -254,10 +258,10 @@
             if 0 <= step - RELAY <= AHEAD:
                 relay(step - RELAY, kind)
             if 0 <= step - PREPARE <= AHEAD:
-                each(step - PREPARE, kind, prepare)
+                each(step - PREPARE, kind, lambda k, slot, sub: prepare(k, slot, sub, kind))
 
     def hand_over():
-        target = device(friend, plane, share)
+        target = device(friend, plane, y_share)
         return remote(raw.at[plane, share], raw.at[plane + KEPT, share], h_send, h_recv, target)
 
     @pl.when(plane < first)
@@ -319,7 +323,7 @@
 
     @pl.when(plane < helped)
     def _():
-        remote(raw.at[0, 0], raw.at[0, 0], h_send, h_recv, device(friend, plane, share)).wait_recv()
+        remote(raw.at[0, 0], raw.at[0, 0], h_send, h_recv, device(friend, plane, y_share)).wait_recv()
 
     gather(1)
 
@@ -508,13 +512,13 @@
     for kind in range(2):
         for distance in range(AHEAD + 1):
             def drained(k, slot, sub):
-                y_copy(slot, sub).wait_send()
-                c_copy(slot, sub, 0).wait_send()
-                c_copy(slot, sub, 1).wait_send()
+                y_copy(slot, sub, kind).wait_send()
+                c_copy(slot, sub, 0, kind).wait_send()
+                c_copy(slot, sub, 1, kind).wait_send()
 
             each(distance, kind, drained)
             for sub in range(CUTS):
-                sends(distance, sub, kind, lambda k, slot, i, way: z_copy(slot, i, way).wait_send())
+                sends(distance, sub, kind, lambda k, slot, i, way: z_copy(slot, i, way, kind).wait_send())
 
     @pl.when(plane < first)
     def _():

time: 102 us -> 101 us (level)
  no operation moved by 1% of the time
where the time goes in v4:
time: 101 us
  Pallas kernels  98.9 us (98%)
  local copies, waits for them, and re-layouts  1.67 us (2%)
    pallas_call x1, Pallas kernels, shards(): pl.pallas_call(kernel, out_shape=jax.ShapeDtypeStruct((ROWS, WIDTH), f32)...  98.9 us

profile of v4, /device:TPU:41, one launch (start us, length us, event | category | flops | bytes accessed | tf_op | source)
XLA Modules:
  0.0 100.5 jit_solution(16038078928795537320)
XLA Ops:
  0.0 98.9 %selected_inverse.1 = f32[128,512]{1,0:T(8,128)} custom-call(f32[128,512]{1,0:T(8,128)} %bitcast.5, f32[512,512]{1,0:T(8,128)} %bitcast.3, s32[8,7]{1,0:T(8,128)} %lists_hbm.1, s32[8]{0:T(128)} %parent_hbm.1), custom_call_target="tpu_custom_call" | custom-call | tf_op jit(solution)/shard_map/selected_inverse/pallas_call | solution.py:591
  98.9 1.7 %copy.6 = f32[1,128,512]{2,1,0:T(8,128)} copy(f32[1,128,512]{2,1,0:T(8,128)} %bitcast.4) | data formatting | bytes 524288

commit v5 on v4

--- a/solution.py
+++ b/solution.py
@@ -420,9 +420,10 @@
 
     kept, sent = upper, 1 - upper
 
-    def x_copy():
+    def x_copy(sub):
         target = device(node, mirror, share)
-        return remote(scaled.at[sent], xrecv, x_send, x_recv, target)
+        rows = pl.ds(sub * PIECE, PIECE)
+        return remote(scaled.at[sent, rows], xrecv.at[rows], x_send.at[sub], x_recv.at[sub], target)
 
     def a_copy(h):
         target = device(node, node, share)
@@ -447,7 +448,8 @@
 
     @pl.when(node >= mirror)
     def _():
-        x_copy().start()
+        for sub in range(SUBS):
+            x_copy(sub).start()
 
     for h in range(2):
         @pl.when(jnp.logical_and(node > blocks[h], node <= DIRECT))
@@ -466,8 +468,9 @@
     @pl.when(node >= plane)
     def _():
         out_ref[pl.ds(upper * HALF, HALF)] = scaled[kept]
-        x_copy().wait_recv()
-        out_ref[pl.ds((1 - upper) * HALF, HALF)] = xrecv[...]
+        for sub in range(SUBS):
+            x_copy(sub).wait_recv()
+            out_ref[pl.ds((1 - upper) * HALF + sub * PIECE, PIECE)] = xrecv[sub * PIECE : (sub + 1) * PIECE]
 
     @pl.when(jnp.logical_and(node == plane, node > DIRECT))
     def _():
@@ -497,7 +500,8 @@
 
     @pl.when(node >= mirror)
     def _():
-        x_copy().wait_send()
+        for sub in range(SUBS):
+            x_copy(sub).wait_send()
 
     @pl.when(jnp.logical_and(node == plane, node > DIRECT))
     def _():
@@ -601,7 +605,7 @@
             messages, pltpu.VMEM((SHARES, 2, HALF, ROWS), f32),
             pair, half, half, half,
             dma((4,)), cuts, row_cuts, row_cuts, row_cuts, cuts, cuts, *[dma(())] * 6,
-            flags, flags, flags, flags, dma(()), dma(()), dma((2,)), dma((NODES, 2)),
+            flags, flags, flags, flags, dma((SUBS,)), dma((SUBS,)), dma((2,)), dma((NODES, 2)),
             dma((NODES, 2, SHARES)), dma((SHARES, 2)),
         ],
         compiler_params=pltpu.CompilerParams(

time: 101 us -> 101 us (level)
  no operation moved by 1% of the time
where the time goes in v5:
time: 101 us
  Pallas kernels  98.9 us (98%)
  local copies, waits for them, and re-layouts  1.67 us (2%)
    pallas_call x1, Pallas kernels, shards(): pl.pallas_call(kernel, out_shape=jax.ShapeDtypeStruct((ROWS, WIDTH), f32)...  98.9 us

profile of v5, /device:TPU:41, one launch (start us, length us, event | category | flops | bytes accessed | tf_op | source)
XLA Modules:
  0.0 100.6 jit_solution(17318968925958702654)
XLA Ops:
  0.0 98.9 %selected_inverse.1 = f32[128,512]{1,0:T(8,128)} custom-call(f32[128,512]{1,0:T(8,128)} %bitcast.5, f32[512,512]{1,0:T(8,128)} %bitcast.3, s32[8,7]{1,0:T(8,128)} %lists_hbm.1, s32[8]{0:T(128)} %parent_hbm.1), custom_call_target="tpu_custom_call" | custom-call | tf_op jit(solution)/shard_map/selected_inverse/pallas_call | solution.py:595
  98.9 1.7 %copy.6 = f32[1,128,512]{2,1,0:T(8,128)} copy(f32[1,128,512]{2,1,0:T(8,128)} %bitcast.4) | data formatting | bytes 524288
